TPU v7x, 32 devices: a whole 2x2x4 slice. The times are simulated.
32 devices in a mesh: grp: 2 (over y), tok: 8 (over z, core), head: 2 (over x).
Axes of the slice: x: 2, y: 2, z: 4, core: 2. Of those that a mesh axis runs over, the one named last changes fastest.
Arguments:
- queries: bfloat16 [2, 8192, 1280], P(None, ('grp', 'tok'), 'head'), parts along dimension 1, may hold values from -6 to 6
- key_tokens: bfloat16 [2, 8192, 1280], P(None, ('grp', 'tok'), 'head'), parts along dimension 1, may hold values from -6 to 6
- values: bfloat16 [2, 8192, 1280], P(None, ('grp', 'tok'), 'head'), parts along dimension 1, may hold values from -6 to 6
- learn_rates: float32 [2, 2, 8192], P(None, 'head', ('grp', 'tok')), parts along dimension 2, may hold values from 0.03 to 0.3
- w_first: float32 [2, 640, 640], P('head'), may hold values from -0.25 to 0.25
- w_second: float32 [2, 640, 640], P('head'), may hold values from -0.25 to 0.25
- w_third: float32 [2, 640, 640], P('head'), may hold values from -0.25 to 0.25
Outputs:
- layer_output: bfloat16 [2, 8192, 1280], P(None, ('grp', 'tok', 'head')), parts along dimension 1
There are 2 independent parts, one for each index of `grp`. A program takes and returns all parts, laid end to end along the dimension named above; an argument that names none is the same for every part. Nothing has to cross between parts.
All inputs are finite; a program needn't handle non-finite values.
Results may differ from a plain program's by a relative error of at most 0.038.
Values may be sent and summed in bfloat16 or wider, within the bound.
A program may use at most 64 MiB of HBM per device.

v0:
```python
import math

import jax
import jax.numpy as jnp
from jax import lax
from jax.sharding import PartitionSpec as P

MOMENTUM_DECAY = 0.9
EPSILON = 1e-06
CONTRACT_ROWS = (((0,), (0,)), ((), ()))
CONTRACT_LAST = (((1,), (1,)), ((), ()))


def silu_slope(pre_act):
    sigmoid_value = jax.nn.sigmoid(pre_act)
    return sigmoid_value * (1.0 + pre_act * (1.0 - sigmoid_value))


def row_rms(matrix):
    return jnp.sqrt(jnp.mean(matrix * matrix, axis=-1, keepdims=True) + EPSILON)


def block_terms(keys_now, values_now, rates_now, first_b, second_b, third_b):
    pre_gate = lax.dot_general(keys_now, first_b, CONTRACT_LAST, preferred_element_type=jnp.float32)
    pre_up = lax.dot_general(keys_now, third_b, CONTRACT_LAST, preferred_element_type=jnp.float32)
    hidden = (jax.nn.silu(pre_gate) * pre_up).astype(jnp.bfloat16)
    scaled = (rates_now[:, None] * values_now.astype(jnp.float32)).astype(jnp.bfloat16)
    back_prop = jnp.dot(scaled, second_b, preferred_element_type=jnp.float32)
    grad_gate = (back_prop * pre_up * silu_slope(pre_gate)).astype(jnp.bfloat16)
    grad_up = (back_prop * jax.nn.silu(pre_gate)).astype(jnp.bfloat16)
    return (hidden, scaled, grad_gate, grad_up)


def weight_grads(gate_part, scaled_part, up_part, keys_now, hidden):
    grad_first = lax.dot_general(
        gate_part, keys_now, CONTRACT_ROWS, preferred_element_type=jnp.float32
    )
    grad_second = lax.dot_general(
        scaled_part, hidden, CONTRACT_ROWS, preferred_element_type=jnp.float32
    )
    grad_third = lax.dot_general(
        up_part, keys_now, CONTRACT_ROWS, preferred_element_type=jnp.float32
    )
    return (grad_first, grad_second, grad_third)


def apply_weights(queries_now, first_b, second_b, third_b):
    pre_gate = lax.dot_general(
        queries_now, first_b, CONTRACT_LAST, preferred_element_type=jnp.float32
    )
    pre_up = lax.dot_general(
        queries_now, third_b, CONTRACT_LAST, preferred_element_type=jnp.float32
    )
    hidden = (jax.nn.silu(pre_gate) * pre_up).astype(jnp.bfloat16)
    return lax.dot_general(
        hidden, second_b, CONTRACT_LAST, preferred_element_type=jnp.float32
    ).astype(jnp.bfloat16)


def local(queries, key_tokens, values, learn_rates, w_first, w_second, w_third):
    inner_width = w_first.shape[1]
    tok_count = lax.axis_size("tok")
    tok_place = lax.axis_index("tok")
    row_share = inner_width // tok_count
    grad_scale = 1.0 / math.sqrt(key_tokens.shape[1] * tok_count)
    rounded = (
        w_first[0].astype(jnp.bfloat16),
        w_second[0].astype(jnp.bfloat16),
        w_third[0].astype(jnp.bfloat16),
    )
    stacked = jnp.stack([w_first[0], w_second[0], w_third[0]], axis=1)
    current = lax.dynamic_slice_in_dim(stacked, tok_place * row_share, row_share, 0)
    target_rms = row_rms(current)
    moment = jnp.zeros_like(current)
    results = []
    for block_index in range(queries.shape[0]):
        keys_now = key_tokens[block_index]
        hidden, scaled, grad_gate, grad_up = block_terms(
            keys_now,
            values[block_index],
            learn_rates[block_index, 0],
            rounded[0],
            rounded[1],
            rounded[2],
        )
        grads = weight_grads(grad_gate, scaled, grad_up, keys_now, hidden)
        row_terms = lax.psum_scatter(
            (jnp.concatenate(grads, axis=1) * grad_scale).astype(jnp.bfloat16),
            "tok",
            scatter_dimension=0,
            tiled=True,
        ).astype(jnp.float32)
        update = row_terms.reshape(row_share, 3, inner_width)
        moment = MOMENTUM_DECAY * moment + update
        summed = current + moment
        current = summed * target_rms / row_rms(summed)
        gathered = lax.all_gather(current.astype(jnp.bfloat16), "tok", axis=0, tiled=True)
        rounded = (gathered[:, 0], gathered[:, 1], gathered[:, 2])
        produced = apply_weights(queries[block_index], rounded[0], rounded[1], rounded[2])
        results.append(lax.all_to_all(produced, "head", split_axis=0, concat_axis=1, tiled=True))
    return jnp.stack(results)


def solution(mesh):
    placed = (
        P(None, ("grp", "tok"), "head"),
        P(None, ("grp", "tok"), "head"),
        P(None, ("grp", "tok"), "head"),
        P(None, "head", ("grp", "tok")),
        P("head", None, None),
        P("head", None, None),
        P("head", None, None),
    )
    return jax.shard_map(
        local,
        mesh=mesh,
        in_specs=placed,
        out_specs=P(None, ("grp", "tok", "head"), None),
        check_vma=False,
    )
```

profile of v0, /device:TPU:0, one launch (start us, length us, event | category | flops | bytes accessed | tf_op | source)
XLA Modules:
  0.0 204.9 jit_solution(682516407225353056)
XLA Ops:
  7.2 2.6 %fusion.14 = f32[512,640]{1,0:T(8,128)S(1)} fusion(f32[1,640,640]{2,1,0:T(8,128)} %param.11, bf16[2,512,640]{2,1,0:T(8,128)(2,1)} %param.8), kind=kOutput, calls=%fused_computation.46 | convolution fusion | flops 419840000 | bytes 3604480 | tf_op jit(solution)/shard_map/dot_general | solution.py:24
  12.5 0.9 fusion.24
  13.4 0.9 fusion.46
  15.5 3.0 %copy.30 = bf16[640,1920]{1,0:T(8,128)(2,1)} copy(bf16[640,1920]{0,1:T(8,128)(2,1)S(1)} %fusion) | data formatting | bytes 4915200
  18.6 39.5 %reduce-scatter.7.cloned.1.call-done = bf16[80,1920]{1,0:T(8,128)(2,1)} async-done(((bf16[640,1920]{1,0:T(8,128)(2,1)}), bf16[80,1920]{1,0:T(8,128)(2,1)}) %reduce-scatter.7.cloned.1.call-update) | async-done | bytes 307216
  58.2 1.2 copy.31
  59.6 1.2 multiply_reduce_fusion.2
  61.7 0.9 fusion.80
  62.7 31.8 %all-gather.3.cloned.1.call-done = bf16[640,3,640]{2,0,1:T(8,128)(2,1)} async-done(((bf16[80,3,640]{2,0,1:T(8,128)(2,1)}), bf16[640,3,640]{2,0,1:T(8,128)(2,1)}) %all-gather.3.cloned.1.call-update) | async-done | bytes 2457616 | tf_op jit(solution)/shard_map/all_gather | solution.py:97
  94.5 2.1 %convolution_bitcast_fusion.2 = f32[512,640]{1,0:T(8,128)S(1)} fusion(bf16[640,3,640]{2,0,1:T(8,128)(2,1)} %all-gather.3.cloned.1.call-done, bf16[2,512,640]{2,1,0:T(8,128)(2,1)S(1)} %copy-done.6), kind=kOutput, calls=%fused_computation.14 | convolution fusion | flops 419430400 | bytes 2785280 | tf_op jit(solution)/shard_map/dot_general | solution.py:24
  99.5 0.9 fusion.38
  101.7 3.1 %copy.32 = bf16[640,1920]{1,0:T(8,128)(2,1)} copy(bf16[640,1920]{0,1:T(8,128)(2,1)S(1)} %fusion.1) | data formatting | bytes 4915200
  105.0 35.9 %reduce-scatter.9.cloned.1.call-done = bf16[80,1920]{1,0:T(8,128)(2,1)} async-done(((bf16[640,1920]{1,0:T(8,128)(2,1)}), bf16[80,1920]{1,0:T(8,128)(2,1)}) %reduce-scatter.9.cloned.1.call-update) | async-done | bytes 307216
  140.9 1.2 copy.33
  142.8 0.9 divide_convert_fusion
  143.7 3.3 %convolution_bitcast_fusion.5 = f32[512,640]{1,0:T(8,128)} fusion(bf16[640,3,640]{2,0,1:T(8,128)(2,1)} %all-gather.3.cloned.1.call-done, bf16[2,512,640]{2,1,0:T(8,128)(2,1)} %param.7), kind=kOutput, calls=%fused_computation.18 | convolution fusion | flops 419430400 | bytes 2785280 | tf_op jit(solution)/shard_map/dot_general | solution.py:48
  147.0 3.7 %convolution_convert_fusion.1 = bf16[512,640]{1,0:T(8,128)(2,1)} fusion(f32[512,640]{1,0:T(8,128)} %convolution_bitcast_fusion.5, bf16[640,3,640]{2,0,1:T(8,128)(2,1)S(1)} %copy-done.10, bf16[2,512,640]{2,1,0:T(8,128)(2,1)} %param.7), kind=kOutput, calls=%fused_computation.22 | convolution fusion | flops 841154560 | bytes 4259840 | tf_op jit(solution)/shard_map/dot_general | solution.py:55
  150.7 3.5 %all-to-all-start = ((bf16[2,256,640]{2,1,0:T(8,128)(2,1)}), bf16[2,256,640]{2,1,0:T(8,128)(2,1)S(1)}, u32[]{:S(2)}, u32[]{:S(2)}) async-start(bf16[2,256,640]{2,1,0:T(8,128)(2,1)} %bitcast.17), calls=%async_computation | async-start | bytes 1310720 | tf_op jit(solution)/shard_map/all_to_all | solution.py:100
  154.3 21.3 %all-gather.5.cloned.1.call-done = bf16[640,3,640]{2,0,1:T(8,128)(2,1)} async-done(((bf16[80,3,640]{2,0,1:T(8,128)(2,1)}), bf16[640,3,640]{2,0,1:T(8,128)(2,1)}) %all-gather.5.cloned.1.call-update) | async-done | bytes 2457616 | tf_op jit(solution)/shard_map/all_gather | solution.py:97
  175.5 3.3 %convolution_bitcast_fusion.1 = f32[512,640]{1,0:T(8,128)} fusion(bf16[640,3,640]{2,0,1:T(8,128)(2,1)} %all-gather.5.cloned.1.call-done, bf16[2,512,640]{2,1,0:T(8,128)(2,1)} %param.7), kind=kOutput, calls=%fused_computation.13 | convolution fusion | flops 419430400 | bytes 2785280 | tf_op jit(solution)/shard_map/dot_general | solution.py:48
  178.8 3.7 %convolution_convert_fusion = bf16[512,640]{1,0:T(8,128)(2,1)} fusion(f32[512,640]{1,0:T(8,128)} %convolution_bitcast_fusion.1, bf16[640,3,640]{2,0,1:T(8,128)(2,1)S(1)} %copy-done.11, bf16[2,512,640]{2,1,0:T(8,128)(2,1)} %param.7), kind=kOutput, calls=%fused_computation.21 | convolution fusion | flops 841154560 | bytes 4259840 | tf_op jit(solution)/shard_map/dot_general | solution.py:55
  182.6 3.5 %all-to-all-start.1 = ((bf16[2,256,640]{2,1,0:T(8,128)(2,1)}), bf16[2,256,640]{2,1,0:T(8,128)(2,1)S(1)}, u32[]{:S(2)}, u32[]{:S(2)}) async-start(bf16[2,256,640]{2,1,0:T(8,128)(2,1)} %bitcast.33), calls=%async_computation.1 | async-start | bytes 1310720 | tf_op jit(solution)/shard_map/all_to_all | solution.py:100
  187.2 8.9 %all-to-all-done.1 = bf16[2,256,640]{2,1,0:T(8,128)(2,1)S(1)} async-done(((bf16[2,256,640]{2,1,0:T(8,128)(2,1)}), bf16[2,256,640]{2,1,0:T(8,128)(2,1)S(1)}, u32[]{:S(2)}, u32[]{:S(2)}) %all-to-all-start.1) | async-done | bytes 655392 | tf_op jit(solution)/shard_map/all_to_all | solution.py:100
  197.2 1.2 pad_maximum_fusion
  (52 shorter events, 12.8 us)
Async XLA Ops:
  6.5 51.6 %reduce-scatter.7.cloned.1.call-start = ((), (), s32[]{:S(2)}) async-start(), calls=%async_computation.6 | async-start | bytes 2764800
  7.2 2.6 %copy-start.1 = (f32[1,640,640]{2,1,0:T(8,128)S(1)}, f32[1,640,640]{2,1,0:T(8,128)}, u32[]{:S(2)}) copy-start(f32[1,640,640]{2,1,0:T(8,128)} %param.13) | copy-start | bytes 4915204
  7.2 2.6 %copy-start.5 = (bf16[2,512,640]{2,1,0:T(8,128)(2,1)S(1)}, bf16[2,512,640]{2,1,0:T(8,128)(2,1)}, u32[]{:S(2)}) copy-start(bf16[2,512,640]{2,1,0:T(8,128)(2,1)} %param.8) | copy-start | bytes 3932164
  9.8 1.4 copy-start.2
  9.8 1.8 copy-start.7
  18.6 41.1 %copy-start = (f32[1,640,640]{2,1,0:T(8,128)S(1)}, f32[1,640,640]{2,1,0:T(8,128)}, u32[]{:S(2)}) copy-start(f32[1,640,640]{2,1,0:T(8,128)} %param.11) | copy-start | bytes 4915204
  18.6 75.9 %all-gather.3.cloned.1.call-start = ((), (), s32[]{:S(2)}) async-start(), calls=%async_computation.4 | async-start | bytes 2764800 | tf_op jit(solution)/shard_map/all_gather | solution.py:97
  60.9 0.8 copy-start.3
  60.9 33.6 %copy-start.6 = (bf16[2,512,640]{2,1,0:T(8,128)(2,1)S(1)}, bf16[2,512,640]{2,1,0:T(8,128)(2,1)}, u32[]{:S(2)}) copy-start(bf16[2,512,640]{2,1,0:T(8,128)(2,1)} %param.8) | copy-start | bytes 3932164
  62.6 78.3 %reduce-scatter.9.cloned.1.call-start = ((), (), s32[]{:S(2)}) async-start(), calls=%async_computation.7 | async-start | bytes 2764800
  94.5 2.1 %copy-start.9 = (bf16[640,3,640]{2,0,1:T(8,128)(2,1)S(1)}, bf16[640,3,640]{2,0,1:T(8,128)(2,1)}, u32[]{:S(2)}) copy-start(bf16[640,3,640]{2,0,1:T(8,128)(2,1)} %all-gather.3.cloned.1.call-done) | copy-start | bytes 7372804
  96.6 1.3 copy-start.8
  104.8 37.6 %copy-start.4 = (f32[80,3,640]{2,0,1:T(8,128)S(1)}, f32[80,3,640]{2,0,1:T(8,128)}, u32[]{:S(2)}) copy-start(f32[80,3,640]{2,0,1:T(8,128)} %copy-done.3) | copy-start | bytes 1843204
  104.8 70.7 %all-gather.5.cloned.1.call-start = ((), (), s32[]{:S(2)}) async-start(), calls=%async_computation.5 | async-start | bytes 2764800 | tf_op jit(solution)/shard_map/all_gather | solution.py:97
  143.7 3.3 %copy-start.10 = (bf16[640,3,640]{2,0,1:T(8,128)(2,1)S(1)}, bf16[640,3,640]{2,0,1:T(8,128)(2,1)}, u32[]{:S(2)}) copy-start(bf16[640,3,640]{2,0,1:T(8,128)(2,1)} %all-gather.3.cloned.1.call-done) | copy-start | bytes 7372804
  150.7 31.8 %all-to-all-start = ((bf16[2,256,640]{2,1,0:T(8,128)(2,1)}), bf16[2,256,640]{2,1,0:T(8,128)(2,1)S(1)}, u32[]{:S(2)}, u32[]{:S(2)}) async-start(bf16[2,256,640]{2,1,0:T(8,128)(2,1)} %bitcast.17), calls=%async_computation | async-start | bytes 1310720 | tf_op jit(solution)/shard_map/all_to_all | solution.py:100
  175.5 3.3 %copy-start.11 = (bf16[640,3,640]{2,0,1:T(8,128)(2,1)S(1)}, bf16[640,3,640]{2,0,1:T(8,128)(2,1)}, u32[]{:S(2)}) copy-start(bf16[640,3,640]{2,0,1:T(8,128)(2,1)} %all-gather.5.cloned.1.call-done) | copy-start | bytes 7372804
  182.6 13.6 %all-to-all-start.1 = ((bf16[2,256,640]{2,1,0:T(8,128)(2,1)}), bf16[2,256,640]{2,1,0:T(8,128)(2,1)S(1)}, u32[]{:S(2)}, u32[]{:S(2)}) async-start(bf16[2,256,640]{2,1,0:T(8,128)(2,1)} %bitcast.33), calls=%async_computation.1 | async-start | bytes 1310720 | tf_op jit(solution)/shard_map/all_to_all | solution.py:100
Sparse Core Ops, SparseCore 0:
  18.7 39.4 reduce-scatter.6
  62.7 31.6 all-gather.2
  104.9 35.9 reduce-scatter.8
  143.8 31.6 all-gather.4
where the time goes:
time: 205 us
  waiting for transfers between devices  137 us (67%)
  matrix products  27.1 us (13%)
  local copies, waits for them, and re-layouts  14.2 us (7%)
  between operations  13.4 us (7%)
  starting transfers between devices  7.33 us (4%)
  other arithmetic  5.36 us (3%)
    unnamed x6, waiting for transfers between devices  75.5 us
    all_gather x2, waiting for transfers between devices, local(): lax.all_gather(current.astype(jnp.bfloat16), 'tok', axis=0, tiled=True)  53.1 us
    unnamed x28, local copies, waits for them, and re-layouts  10.9 us
    all_to_all x2, waiting for transfers between devices, local(): lax.all_to_all(produced, 'head', split_axis=0, concat_axis=1, tiled=True)  8.93 us
    dot_general x2, matrix products, apply_weights(): lax.dot_general(hidden, second_b, CONTRACT_LAST, preferred_element_type=j...  7.47 us
    all_to_all x2, starting transfers between devices, local(): lax.all_to_all(produced, 'head', split_axis=0, concat_axis=1, tiled=True)  7.02 us
    dot_general x2, matrix products, apply_weights(): lax.dot_general(queries_now, first_b, CONTRACT_LAST, preferred_element_ty...  6.63 us
    dot_general x2, matrix products, block_terms(): lax.dot_general(keys_now, first_b, CONTRACT_LAST, preferred_element_type=...  4.64 us
  transfers between devices with their start and end apart: 6, of which 5 were waited for; matrix products, arithmetic and copies ran while one was open for 7% of the time, Pallas kernels for 0%

commit v1 on v0

v1 whole, which is shorter than its diff:
```python
import functools
import math

import jax
import jax.numpy as jnp
from jax import lax
from jax.experimental import pallas as pl
from jax.experimental.pallas import tpu as pltpu
from jax.sharding import PartitionSpec as P

MOMENTUM_DECAY = 0.9
EPSILON = 1e-06
CONTRACT_ROWS = (((0,), (0,)), ((), ()))
CONTRACT_LAST = (((1,), (1,)), ((), ()))
MESH = pl.DeviceIdType.MESH
CORES = 2
GATE, OUT, UP = 0, 1, 2
SPACING = 2


def row_rms(matrix):
    return jnp.sqrt(jnp.mean(matrix * matrix, axis=-1, keepdims=True) + EPSILON)


def dot(lhs, rhs, dims):
    return lax.dot_general(lhs, rhs, dims, preferred_element_type=jnp.float32)


def kernel(
    tok_count, head_count, share, inner,
    q_hbm, k_hbm, v_hbm, rates_ref, w1_hbm, w2_hbm, w3_hbm, out_ref,
    q_ref, k_ref, v_ref, w_ref, weights, silu_s, slope_s, e_s, z_s, ga_s, gb_s,
    grads, pair_in, from_left, from_right, cur_s, mom_s, made,
    load_sem, pair_send, pair_recv, r_send, r_recv, l_send, l_recv,
    agr_send, agl_send, ag_recv, agp_send, agp_recv, out_send, out_recv,
):
    line = tok_count // CORES
    half = line * share
    blocks, tokens, width = q_ref.shape
    slab = tokens // head_count
    tile = min(256, tokens)
    grad_scale = 1.0 / math.sqrt(tokens * tok_count)
    tok = lax.axis_index("tok")
    head = lax.axis_index("head")
    z = tok // CORES
    core = lax.rem(tok, CORES)
    mate = tok + 1 - 2 * core
    has_left = z > 0
    has_right = z < line - 1
    left, right = tok - CORES, tok + CORES

    def rows_of(owner, of_core):
        return pl.ds(pl.multiple_of((of_core * line + owner) * share, share), share)

    def in_half(owner):
        return pl.ds(pl.multiple_of(owner * share, share), share)

    barrier = pltpu.get_barrier_semaphore()

    @pl.when(has_left)
    def _():
        pl.semaphore_signal(barrier, inc=1, device_id={"tok": left}, device_id_type=MESH)

    @pl.when(has_right)
    def _():
        pl.semaphore_signal(barrier, inc=1, device_id={"tok": right}, device_id_type=MESH)

    pl.semaphore_signal(barrier, inc=1, device_id={"tok": mate}, device_id_type=MESH)
    for step in range(1, head_count):
        pl.semaphore_signal(
            barrier, inc=1, device_id={"head": lax.rem(head + step, head_count)}, device_id_type=MESH
        )

    loads = {}
    order = [
        ("k0", k_hbm.at[0], k_ref.at[0]),
        ("w1", w1_hbm, w_ref.at[GATE]),
        ("w3", w3_hbm, w_ref.at[UP]),
        ("v0", v_hbm.at[0], v_ref.at[0]),
        ("w2", w2_hbm, w_ref.at[OUT]),
    ]
    for b in range(1, blocks):
        order.append((f"k{b}", k_hbm.at[b], k_ref.at[b]))
        order.append((f"v{b}", v_hbm.at[b], v_ref.at[b]))
    for b in range(blocks):
        order.append((f"q{b}", q_hbm.at[b], q_ref.at[b]))
    for place, (name, src, dst) in enumerate(order):
        loads[name] = pltpu.make_async_copy(src, dst, load_sem.at[place])
        loads[name].start()

    def round_weights(m):
        weights[0, m] = w_ref[m].astype(jnp.bfloat16)

    def keys_part(b):
        @pl.loop(0, tokens // tile)
        def _(i):
            rows = pl.ds(pl.multiple_of(i * tile, tile), tile)
            keys = k_ref[b, rows]
            gate = dot(keys, weights[b, GATE, :inner], CONTRACT_LAST)
            up = dot(keys, weights[b, UP, :inner], CONTRACT_LAST)
            sig = jax.nn.sigmoid(gate)
            silu = gate * sig
            z_s[rows] = (silu * up).astype(jnp.bfloat16)
            silu_s[rows] = silu
            slope_s[rows] = up * (sig * (1.0 + gate * (1.0 - sig)))

    def scaled_part(b):
        lanes = math.gcd(width, 128)
        for i in range(tokens // tile):
            rows = pl.ds(i * tile, tile)
            rate = jnp.transpose(jnp.broadcast_to(rates_ref[b, :, rows], (lanes, tile)))
            for j in range(width // lanes):
                cols = pl.ds(j * lanes, lanes)
                e_s[rows, cols] = (rate * v_ref[b, rows, cols].astype(jnp.float32)).astype(jnp.bfloat16)

    def back_part(b):
        @pl.loop(0, tokens // tile)
        def _(i):
            rows = pl.ds(pl.multiple_of(i * tile, tile), tile)
            back = lax.dot_general(
                e_s[rows], weights[b, OUT, :inner], (((1,), (0,)), ((), ())),
                preferred_element_type=jnp.float32,
            )
            ga_s[rows] = (back * slope_s[rows]).astype(jnp.bfloat16)
            gb_s[rows] = (back * silu_s[rows]).astype(jnp.bfloat16)

    def grad_part(b, m):
        if m == GATE:
            value = dot(ga_s[...], k_ref[b], CONTRACT_ROWS)
        elif m == OUT:
            value = dot(e_s[...], z_s[...], CONTRACT_ROWS)
        else:
            value = dot(gb_s[...], k_ref[b], CONTRACT_ROWS)
        grads[b, m, :inner] = value.astype(jnp.bfloat16)
        if CORES * half > inner:
            grads[b, m, inner:] = jnp.zeros((CORES * half - inner, width), jnp.bfloat16)

    def pair_copy(b, m):
        other = pl.ds(pl.multiple_of((1 - core) * half, half), half)
        return pltpu.make_async_remote_copy(
            src_ref=grads.at[b, m, other], dst_ref=pair_in.at[b, m],
            send_sem=pair_send.at[b * 3 + m], recv_sem=pair_recv.at[b * 3 + m],
            device_id={"tok": mate}, device_id_type=MESH,
        )

    def line_copy(buf, b, m, owner, send, recv, to):
        return pltpu.make_async_remote_copy(
            src_ref=buf.at[b, m, in_half(owner)], dst_ref=buf.at[b, m, in_half(owner)],
            send_sem=send.at[b * 3 + m, owner], recv_sem=recv.at[b * 3 + m, owner],
            device_id={"tok": to}, device_id_type=MESH,
        )

    def right_copy(b, m, owner):
        return line_copy(from_left, b, m, owner, r_send, r_recv, right)

    def left_copy(b, m, owner):
        return line_copy(from_right, b, m, owner, l_send, l_recv, left)

    def share_copy(b, m, owner, of_core, send, recv, to):
        place = weights.at[b + 1, m, rows_of(owner, of_core)]
        return pltpu.make_async_remote_copy(
            src_ref=place, dst_ref=place,
            send_sem=send.at[b * 3 + m, owner], recv_sem=recv.at[b * 3 + m, owner],
            device_id={"tok": to}, device_id_type=MESH,
        )

    def own_term(b, m, owner):
        return (
            grads[b, m, rows_of(owner, core)].astype(jnp.float32)
            + pair_in[b, m, in_half(owner)].astype(jnp.float32)
        )

    def reduce_step(b, m, t):
        if t < line - 1:
            @pl.when(z <= t)
            def _():
                owner = line - 1 - t + z
                value = own_term(b, m, owner)

                @pl.when(z == 0)
                def _():
                    from_left[b, m, in_half(owner)] = value.astype(jnp.bfloat16)

                @pl.when(z > 0)
                def _():
                    right_copy(b, m, owner).wait_recv()
                    from_left[b, m, in_half(owner)] = (
                        value + from_left[b, m, in_half(owner)].astype(jnp.float32)
                    ).astype(jnp.bfloat16)

                right_copy(b, m, owner).start()

            @pl.when(line - 1 - z <= t)
            def _():
                owner = t - (line - 1) + z
                value = own_term(b, m, owner)

                @pl.when(z == line - 1)
                def _():
                    from_right[b, m, in_half(owner)] = value.astype(jnp.bfloat16)

                @pl.when(z < line - 1)
                def _():
                    left_copy(b, m, owner).wait_recv()
                    from_right[b, m, in_half(owner)] = (
                        value + from_right[b, m, in_half(owner)].astype(jnp.float32)
                    ).astype(jnp.bfloat16)

                left_copy(b, m, owner).start()

    def update(b, m):
        @pl.when(has_left)
        def _():
            right_copy(b, m, z).wait_recv()

        @pl.when(has_right)
        def _():
            left_copy(b, m, z).wait_recv()

        mine = in_half(z)

        @pl.when(jnp.logical_not(has_left))
        def _():
            from_left[b, m, mine] = jnp.zeros((share, width), jnp.bfloat16)

        @pl.when(jnp.logical_not(has_right))
        def _():
            from_right[b, m, mine] = jnp.zeros((share, width), jnp.bfloat16)

        total = (
            own_term(b, m, z)
            + from_left[b, m, mine].astype(jnp.float32)
            + from_right[b, m, mine].astype(jnp.float32)
        ) * grad_scale
        first = w_ref[m, rows_of(z, core)]
        if b == 0:
            moment, before = total, first
        else:
            moment, before = MOMENTUM_DECAY * mom_s[m] + total, cur_s[m]
        summed = before + moment
        after = summed * row_rms(first) / row_rms(summed)
        mom_s[m] = moment
        cur_s[m] = after
        weights[b + 1, m, rows_of(z, core)] = after.astype(jnp.bfloat16)

        @pl.when(has_right)
        def _():
            share_copy(b, m, z, core, agr_send, ag_recv, right).start()

        @pl.when(has_left)
        def _():
            share_copy(b, m, z, core, agl_send, ag_recv, left).start()

        share_copy(b, m, z, core, agp_send, agp_recv, mate).start()

    def gather_step(b, m, t):
        @pl.when(z >= t)
        def _():
            owner = z - t
            share_copy(b, m, owner, core, agr_send, ag_recv, right).wait_recv()

            @pl.when(has_right)
            def _():
                share_copy(b, m, owner, core, agr_send, ag_recv, right).start()

            share_copy(b, m, owner, core, agp_send, agp_recv, mate).start()

        @pl.when(z + t <= line - 1)
        def _():
            owner = z + t
            share_copy(b, m, owner, core, agl_send, ag_recv, left).wait_recv()

            @pl.when(has_left)
            def _():
                share_copy(b, m, owner, core, agl_send, ag_recv, left).start()

            share_copy(b, m, owner, core, agp_send, agp_recv, mate).start()

    def gather_end(b, m):
        for owner in range(line):
            share_copy(b, m, owner, 1 - core, agp_send, agp_recv, mate).wait_recv()

    def chunk_steps(b, m):
        def begin():
            pair_copy(b, m).wait_recv()
            reduce_step(b, m, 0)

        steps = [begin]
        steps += [functools.partial(reduce_step, b, m, t) for t in range(1, line - 1)]
        steps.append(functools.partial(update, b, m))
        steps += [functools.partial(gather_step, b, m, t) for t in range(1, line)]
        steps.append(functools.partial(gather_end, b, m))
        return steps

    def out_copy(b, to):
        return pltpu.make_async_remote_copy(
            src_ref=made.at[b, pl.ds(pl.multiple_of(to * slab, slab), slab)],
            dst_ref=out_ref.at[b, :, pl.ds(pl.multiple_of(head * width, width), width)],
            send_sem=out_send.at[b, to], recv_sem=out_recv.at[b, head],
            device_id={"head": to}, device_id_type=MESH,
        )

    def out_arrival(b, source):
        return pltpu.make_async_remote_copy(
            src_ref=made.at[b, pl.ds(0, slab)],
            dst_ref=out_ref.at[b, :, pl.ds(pl.multiple_of(source * width, width), width)],
            send_sem=out_send.at[b, source], recv_sem=out_recv.at[b, source],
            device_id={"head": source}, device_id_type=MESH,
        )

    def out_own(b):
        return pltpu.make_async_copy(
            made.at[b, pl.ds(pl.multiple_of(head * slab, slab), slab)],
            out_ref.at[b, :, pl.ds(pl.multiple_of(head * width, width), width)],
            out_send.at[b, head],
        )

    def out_part(b, step):
        to = lax.rem(head + step, head_count)
        rows = pl.ds(pl.multiple_of(to * slab, slab), slab)
        query = q_ref[b, rows]
        gate = dot(query, weights[b + 1, GATE, :inner], CONTRACT_LAST)
        up = dot(query, weights[b + 1, UP, :inner], CONTRACT_LAST)
        hidden = (jax.nn.silu(gate) * up).astype(jnp.bfloat16)
        made[b, rows] = dot(hidden, weights[b + 1, OUT, :inner], CONTRACT_LAST).astype(jnp.bfloat16)
        if step < head_count:
            out_copy(b, to).start()
        else:
            out_own(b).start()

    active = []

    def tick():
        for steps in list(active):
            steps.pop(0)()
            if not steps:
                active.remove(steps)

    def launch(b, m):
        grad_part(b, m)
        pair_copy(b, m).start()
        steps = chunk_steps(b, m)
        active.append(steps)
        return steps

    for name in ("k0", "w1", "w3"):
        loads[name].wait()
    round_weights(GATE)
    round_weights(UP)
    keys_part(0)
    loads["v0"].wait()
    scaled_part(0)
    loads["w2"].wait()
    round_weights(OUT)
    back_part(0)

    ends = jnp.where(has_left, 1, 0) + jnp.where(has_right, 1, 0)
    pl.semaphore_wait(barrier, head_count + ends)

    parts_left = []
    for b in range(blocks):
        if b == 0:
            plan = (GATE, UP, OUT)
            chunks = {}
            for place, m in enumerate(plan):
                if place:
                    for _ in range(SPACING):
                        tick()
                chunks[m] = launch(b, m)
        else:
            while chunks[GATE] or chunks[UP]:
                tick()
            loads[f"k{b}"].wait()
            loads[f"v{b}"].wait()
            keys_part(b)
            scaled_part(b)
            before, chunks = chunks, {}
            chunks[OUT] = launch(b, OUT)
            while before[OUT]:
                tick()
            back_part(b)
            chunks[GATE] = launch(b, GATE)
            loads[f"q{b - 1}"].wait()
            parts_left = [functools.partial(out_part, b - 1, step) for step in range(1, head_count + 1)]
            for _ in range(SPACING):
                tick()
                if parts_left:
                    parts_left.pop(0)()
            chunks[UP] = launch(b, UP)
            while parts_left:
                tick()
                parts_left.pop(0)()
    while active:
        tick()
    loads[f"q{blocks - 1}"].wait()
    for step in range(1, head_count + 1):
        out_part(blocks - 1, step)

    for b in range(blocks):
        for m in range(3):
            pair_copy(b, m).wait_send()
            for owner in range(line):
                @pl.when(jnp.logical_and(has_right, owner > z))
                def _():
                    right_copy(b, m, owner).wait_send()

                @pl.when(jnp.logical_and(has_left, owner < z))
                def _():
                    left_copy(b, m, owner).wait_send()

                @pl.when(jnp.logical_and(has_right, owner <= z))
                def _():
                    share_copy(b, m, owner, core, agr_send, ag_recv, right).wait_send()

                @pl.when(jnp.logical_and(has_left, owner >= z))
                def _():
                    share_copy(b, m, owner, core, agl_send, ag_recv, left).wait_send()

                share_copy(b, m, owner, core, agp_send, agp_recv, mate).wait_send()
        out_own(b).wait()
        for step in range(1, head_count):
            other = lax.rem(head + step, head_count)
            out_copy(b, other).wait_send()
            out_arrival(b, other).wait_recv()


def local(tok_count, head_count, queries, key_tokens, values, learn_rates, w_first, w_second, w_third):
    blocks, tokens, width = queries.shape
    inner = w_first.shape[1]
    line = tok_count // CORES
    share = -(-inner // (tok_count * 16)) * 16
    padded = share * tok_count
    half = share * line
    firsts = [w[0] for w in (w_first, w_second, w_third)]
    if padded > inner:
        firsts = [jnp.pad(w, ((0, padded - inner), (0, 0))) for w in firsts]
    bf16, f32 = jnp.bfloat16, jnp.float32
    dma = pltpu.SemaphoreType.DMA
    body = functools.partial(kernel, tok_count, head_count, share, inner)
    hbm = pl.BlockSpec(memory_space=pl.ANY)
    return pl.pallas_call(
        body,
        out_shape=jax.ShapeDtypeStruct((blocks, tokens // head_count, width * head_count), bf16),
        in_specs=[hbm, hbm, hbm, pl.BlockSpec(memory_space=pltpu.VMEM), hbm, hbm, hbm],
        out_specs=hbm,
        scratch_shapes=[
            pltpu.VMEM((blocks, tokens, width), bf16),
            pltpu.VMEM((blocks, tokens, width), bf16),
            pltpu.VMEM((blocks, tokens, width), bf16),
            pltpu.VMEM((3, padded, width), f32),
            pltpu.VMEM((blocks + 1, 3, padded, width), bf16),
            pltpu.VMEM((tokens, inner), f32),
            pltpu.VMEM((tokens, inner), f32),
            pltpu.VMEM((tokens, width), bf16),
            pltpu.VMEM((tokens, inner), bf16),
            pltpu.VMEM((tokens, inner), bf16),
            pltpu.VMEM((tokens, inner), bf16),
            pltpu.VMEM((blocks, 3, padded, width), bf16),
            pltpu.VMEM((blocks, 3, half, width), bf16),
            pltpu.VMEM((blocks, 3, half, width), bf16),
            pltpu.VMEM((blocks, 3, half, width), bf16),
            pltpu.VMEM((3, share, width), f32),
            pltpu.VMEM((3, share, width), f32),
            pltpu.VMEM((blocks, tokens, width), bf16),
            dma((3 + 3 * blocks,)),
            dma((3 * blocks,)),
            dma((3 * blocks,)),
        ]
        + [dma((3 * blocks, line)) for _ in range(9)]
        + [dma((blocks, head_count)) for _ in range(2)],
        compiler_params=pltpu.CompilerParams(
            collective_id=0, has_side_effects=True, vmem_limit_bytes=56 * 1024 * 1024
        ),
    )(queries, key_tokens, values, learn_rates, *firsts)


def solution(mesh):
    placed = (
        P(None, ("grp", "tok"), "head"),
        P(None, ("grp", "tok"), "head"),
        P(None, ("grp", "tok"), "head"),
        P(None, "head", ("grp", "tok")),
        P("head", None, None),
        P("head", None, None),
        P("head", None, None),
    )
    return jax.shard_map(
        functools.partial(local, mesh.shape["tok"], mesh.shape["head"]),
        mesh=mesh,
        in_specs=placed,
        out_specs=P(None, ("grp", "tok", "head"), None),
        check_vma=False,
    )
```

time: 205 us -> 117 us (0.57)
  waiting for transfers between devices: 137 us -> 0 us
  Pallas kernels: 0 us -> 115 us
  matrix products: 27.1 us -> 0 us
  between operations: 13.4 us -> 0.01 us
  local copies, waits for them, and re-layouts: 14.2 us -> 2.46 us
  starting transfers between devices: 7.33 us -> 0 us
  other arithmetic: 5.36 us -> 0 us
    pallas_call x0 -> x1, Pallas kernels: none -> 115 us  [local(): pl.pallas_call(body, out_shape=jax.ShapeDtypeStruct((blocks, tokens // he...]
    unnamed x6 -> x0, waiting for transfers between devices: 75.5 us -> none
    all_gather x2 -> x0, waiting for transfers between devices: 53.1 us -> none  [local(): lax.all_gather(current.astype(jnp.bfloat16), 'tok', axis=0, tiled=True)]
    dot_general x16 -> x0, matrix products: 27.1 us -> none  [the longest x2 7.47 us: apply_weights(): lax.dot_general(hidden, second_b, CONTRACT_LAST, preferred_element_type=j...]
    all_to_all x2 -> x0, waiting for transfers between devices: 8.93 us -> none  [local(): lax.all_to_all(produced, 'head', split_axis=0, concat_axis=1, tiled=True)]
    unnamed x28 -> x1, local copies, waits for them, and re-layouts: 10.9 us -> 2.46 us
    all_to_all x2 -> x0, starting transfers between devices: 7.02 us -> none  [local(): lax.all_to_all(produced, 'head', split_axis=0, concat_axis=1, tiled=True)]
    convert_element_type x4 -> x0, other arithmetic: 2.58 us -> none  [the longest x2 1.78 us: local(): current.astype(jnp.bfloat16)]
  transfers between devices with their start and end apart: 6 -> 0, of which waited for: 5 -> 0; matrix products, arithmetic and copies ran while one was open for 7% -> 0% of each run, Pallas kernels for 0% -> 0%
where the time goes in v1:
time: 117 us
  Pallas kernels  115 us (98%)
  local copies, waits for them, and re-layouts  2.46 us (2%)
    pallas_call x1, Pallas kernels, local(): pl.pallas_call(body, out_shape=jax.ShapeDtypeStruct((blocks, tokens // he...  115 us
    unnamed x1, local copies, waits for them, and re-layouts  2.46 us

profile of v1, /device:TPU:0, one launch (start us, length us, event | category | flops | bytes accessed | tf_op | source)
XLA Modules:
  0.0 117.0 jit_solution(1245736646052247257)
XLA Ops:
  0.0 114.5 %shard_map.73 = bf16[2,256,1280]{2,1,0:T(8,128)(2,1)} custom-call(bf16[2,512,640]{2,1,0:T(8,128)(2,1)} %q_hbm.1, bf16[2,512,640]{2,1,0:T(8,128)(2,1)} %k_hbm.1, bf16[2,512,640]{2,1,0:T(8,128)(2,1)} %v_hbm.1, f32[2,1,512]{2,1,0:T(1,128)} %rates_ref.1, f32[640,640]{1,0:T(8,128)} %bitcast.3, f32[640,640]{1,0:T(8,128)} %bitcast.4, f32[640,640]{1,0:T(8,128)} %bitcast.5), custom_call_target="tpu_custom_call" | custom-call | tf_op jit(solution)/shard_map/pallas_call | solution.py:441
  114.5 2.5 %copy.9 = bf16[2,256,1280]{2,1,0:T(8,128)(2,1)} copy(bf16[2,256,1280]{2,1,0:T(8,128)(2,1)} %shard_map.73) | data formatting | bytes 2621440

commit v2 on v0

v2 whole, which is shorter than its diff:
```python
import functools
import math

import jax
import jax.numpy as jnp
from jax import lax
from jax.experimental import pallas as pl
from jax.experimental.pallas import tpu as pltpu
from jax.sharding import PartitionSpec as P

MOMENTUM_DECAY = 0.9
EPSILON = 1e-06
CONTRACT_ROWS = (((0,), (0,)), ((), ()))
CONTRACT_LAST = (((1,), (1,)), ((), ()))
MESH = pl.DeviceIdType.MESH
CORES = 2
GATE, OUT, UP = 0, 1, 2
CHUNKS = 4
LAG = 3


def row_rms(matrix):
    return jnp.sqrt(jnp.mean(matrix * matrix, axis=-1, keepdims=True) + EPSILON)


def dot(lhs, rhs, dims):
    return lax.dot_general(lhs, rhs, dims, preferred_element_type=jnp.float32)


def kernel(
    tok_count, head_count, chunks, pieces, inner,
    q_hbm, k_hbm, v_hbm, rates_ref, w1_hbm, w2_hbm, w3_hbm, out_ref,
    q_ref, k_ref, v_ref, w_ref, weights, silu_s, slope_s, e_s, z_s, ga_s, gb_s,
    grads, pair_in, partial, from_outer, from_cross, cur_s, mom_s, made,
    load_sem, pair_send, pair_recv, in_send, outer_recv, cross_recv,
    w_send, w_recv, m_send, m_recv, out_send, out_recv,
):
    line = tok_count // CORES
    half = inner // CORES
    chunk = half // chunks
    deepest = line // 2 - 1
    blocks, tokens, width = q_ref.shape
    slab = tokens // head_count
    piece = slab // pieces
    tile = min(256, tokens)
    grad_scale = 1.0 / math.sqrt(tokens * tok_count)
    tok = lax.axis_index("tok")
    head = lax.axis_index("head")
    z = tok // CORES
    core = lax.rem(tok, CORES)
    mate = tok + 1 - 2 * core
    is_low = z <= deepest
    depth = jnp.where(is_low, z, line - 1 - z)
    inward = jnp.where(is_low, tok + CORES, tok - CORES)
    outward = jnp.where(is_low, tok - CORES, tok + CORES)

    def rows_of(of_core, c):
        return pl.ds(pl.multiple_of(of_core * half + c * chunk, 16), chunk)

    def in_half(c):
        return pl.ds(c * chunk, chunk)

    barrier = pltpu.get_barrier_semaphore()

    @pl.when(depth > 0)
    def _():
        pl.semaphore_signal(barrier, inc=1, device_id={"tok": outward}, device_id_type=MESH)

    pl.semaphore_signal(barrier, inc=1, device_id={"tok": inward}, device_id_type=MESH)
    pl.semaphore_signal(barrier, inc=1, device_id={"tok": mate}, device_id_type=MESH)
    for step in range(1, head_count):
        pl.semaphore_signal(
            barrier, inc=1, device_id={"head": lax.rem(head + step, head_count)}, device_id_type=MESH
        )

    loads = {}
    order = [
        ("k0", k_hbm.at[0], k_ref.at[0]),
        ("w1", w1_hbm, w_ref.at[GATE]),
        ("w3", w3_hbm, w_ref.at[UP]),
        ("v0", v_hbm.at[0], v_ref.at[0]),
        ("w2", w2_hbm, w_ref.at[OUT]),
    ]
    for b in range(1, blocks):
        order.append((f"k{b}", k_hbm.at[b], k_ref.at[b]))
        order.append((f"v{b}", v_hbm.at[b], v_ref.at[b]))
    for b in range(blocks):
        order.append((f"q{b}", q_hbm.at[b], q_ref.at[b]))
    for place, (name, src, dst) in enumerate(order):
        loads[name] = pltpu.make_async_copy(src, dst, load_sem.at[place])
        loads[name].start()

    def round_weights(m):
        weights[0, m] = w_ref[m].astype(jnp.bfloat16)

    def keys_part(b):
        @pl.loop(0, tokens // tile)
        def _(i):
            rows = pl.ds(pl.multiple_of(i * tile, tile), tile)
            keys = k_ref[b, rows]
            gate = dot(keys, weights[b, GATE], CONTRACT_LAST)
            up = dot(keys, weights[b, UP], CONTRACT_LAST)
            sig = jax.nn.sigmoid(gate)
            silu = gate * sig
            z_s[rows] = (silu * up).astype(jnp.bfloat16)
            silu_s[rows] = silu
            slope_s[rows] = up * (sig * (1.0 + gate * (1.0 - sig)))

    def scaled_part(b):
        lanes = math.gcd(width, 128)
        for i in range(tokens // tile):
            rows = pl.ds(i * tile, tile)
            rate = jnp.transpose(jnp.broadcast_to(rates_ref[b, :, rows], (lanes, tile)))
            for j in range(width // lanes):
                cols = pl.ds(j * lanes, lanes)
                e_s[rows, cols] = (rate * v_ref[b, rows, cols].astype(jnp.float32)).astype(jnp.bfloat16)

    def back_part(b):
        @pl.loop(0, tokens // tile)
        def _(i):
            rows = pl.ds(pl.multiple_of(i * tile, tile), tile)
            back = lax.dot_general(
                e_s[rows], weights[b, OUT], (((1,), (0,)), ((), ())),
                preferred_element_type=jnp.float32,
            )
            ga_s[rows] = (back * slope_s[rows]).astype(jnp.bfloat16)
            gb_s[rows] = (back * silu_s[rows]).astype(jnp.bfloat16)

    def grad_part(b, m):
        if m == GATE:
            value = dot(ga_s[...], k_ref[b], CONTRACT_ROWS)
        elif m == OUT:
            value = dot(e_s[...], z_s[...], CONTRACT_ROWS)
        else:
            value = dot(gb_s[...], k_ref[b], CONTRACT_ROWS)
        grads[b, m] = value.astype(jnp.bfloat16)

    def pair_copy(b, m, c):
        return pltpu.make_async_remote_copy(
            src_ref=grads.at[b, m, rows_of(1 - core, c)], dst_ref=pair_in.at[b, m, in_half(c)],
            send_sem=pair_send.at[b * 3 + m, c], recv_sem=pair_recv.at[b * 3 + m, c],
            device_id={"tok": mate}, device_id_type=MESH,
        )

    def sum_copy(b, m, c, into, recv):
        return pltpu.make_async_remote_copy(
            src_ref=partial.at[b, m, in_half(c)], dst_ref=into.at[b, m, in_half(c)],
            send_sem=in_send.at[b * 3 + m, c], recv_sem=recv.at[b * 3 + m, c],
            device_id={"tok": inward}, device_id_type=MESH,
        )

    def inward_copy(b, m, c):
        return sum_copy(b, m, c, from_outer, outer_recv)

    def cross_copy(b, m, c):
        return sum_copy(b, m, c, from_cross, cross_recv)

    def weight_copy(b, m, c, of_core, send, recv, to):
        place = weights.at[b + 1, m, rows_of(of_core, c)]
        return pltpu.make_async_remote_copy(
            src_ref=place, dst_ref=place,
            send_sem=send.at[b * 3 + m, c], recv_sem=recv.at[b * 3 + m, c],
            device_id={"tok": to}, device_id_type=MESH,
        )

    def outward_copy(b, m, c):
        return weight_copy(b, m, c, core, w_send, w_recv, outward)

    def mate_copy(b, m, c, of_core):
        return weight_copy(b, m, c, of_core, m_send, m_recv, mate)

    def sum_step(b, m, c, t):
        if t == 0:
            pair_copy(b, m, c).wait_recv()

        @pl.when(depth == t)
        def _():
            value = (
                grads[b, m, rows_of(core, c)].astype(jnp.float32)
                + pair_in[b, m, in_half(c)].astype(jnp.float32)
            )
            if t > 0:
                inward_copy(b, m, c).wait_recv()
                value = value + from_outer[b, m, in_half(c)].astype(jnp.float32)
            partial[b, m, in_half(c)] = value.astype(jnp.bfloat16)
            if t == deepest:
                cross_copy(b, m, c).start()
            else:
                inward_copy(b, m, c).start()

    def send_weights(b, m, c):
        @pl.when(depth > 0)
        def _():
            outward_copy(b, m, c).start()

        mate_copy(b, m, c, core).start()

    def update(b, m, c):
        @pl.when(depth == deepest)
        def _():
            cross_copy(b, m, c).wait_recv()
            total = (
                partial[b, m, in_half(c)].astype(jnp.float32)
                + from_cross[b, m, in_half(c)].astype(jnp.float32)
            ) * grad_scale
            first = w_ref[m, rows_of(core, c)]
            if b == 0:
                moment, before = total, first
            else:
                moment = MOMENTUM_DECAY * mom_s[m, in_half(c)] + total
                before = cur_s[m, in_half(c)]
            summed = before + moment
            after = summed * row_rms(first) / row_rms(summed)
            mom_s[m, in_half(c)] = moment
            cur_s[m, in_half(c)] = after
            weights[b + 1, m, rows_of(core, c)] = after.astype(jnp.bfloat16)
            send_weights(b, m, c)

    def weight_step(b, m, c, t):
        @pl.when(depth == deepest - t)
        def _():
            outward_copy(b, m, c).wait_recv()
            send_weights(b, m, c)

    def weight_end(b, m, c):
        mate_copy(b, m, c, 1 - core).wait_recv()

    def chunk_steps(b, m, c):
        steps = [functools.partial(sum_step, b, m, c, t) for t in range(deepest + 1)]
        steps.append(functools.partial(update, b, m, c))
        steps += [functools.partial(weight_step, b, m, c, t) for t in range(1, deepest + 1)]
        steps.append(functools.partial(weight_end, b, m, c))
        return steps

    def out_rows(to, p):
        return pl.ds(pl.multiple_of(to * slab + p * piece, 16), piece)

    def out_place(b, source, p):
        columns = pl.ds(pl.multiple_of(source * width, width), width)
        return out_ref.at[b, pl.ds(p * piece, piece), columns]

    def out_copy(b, to, p):
        return pltpu.make_async_remote_copy(
            src_ref=made.at[b, out_rows(to, p)], dst_ref=out_place(b, head, p),
            send_sem=out_send.at[b * pieces + p, to], recv_sem=out_recv.at[b * pieces + p, head],
            device_id={"head": to}, device_id_type=MESH,
        )

    def out_arrival(b, source, p):
        return pltpu.make_async_remote_copy(
            src_ref=made.at[b, out_rows(source, p)], dst_ref=out_place(b, source, p),
            send_sem=out_send.at[b * pieces + p, source], recv_sem=out_recv.at[b * pieces + p, source],
            device_id={"head": source}, device_id_type=MESH,
        )

    def out_own(b, p):
        return pltpu.make_async_copy(
            made.at[b, out_rows(head, p)], out_place(b, head, p), out_send.at[b * pieces + p, head]
        )

    def query_part(b, i):
        rows = pl.ds(i * tile, tile)
        silu_s[rows] = jax.nn.silu(dot(q_ref[b, rows], weights[b + 1, GATE], CONTRACT_LAST))

    def out_part(b, step, p):
        to = lax.rem(head + step, head_count)
        rows = out_rows(to, p)
        up = dot(q_ref[b, rows], weights[b + 1, UP], CONTRACT_LAST)
        hidden = (silu_s[rows] * up).astype(jnp.bfloat16)
        made[b, rows] = dot(hidden, weights[b + 1, OUT], CONTRACT_LAST).astype(jnp.bfloat16)
        if step < head_count:
            out_copy(b, to, p).start()
        else:
            out_own(b, p).start()

    def out_parts(b):
        return [
            functools.partial(out_part, b, step, p)
            for step in range(1, head_count + 1)
            for p in range(pieces)
        ]

    waiting, active, ended = [], [], set()

    def tick():
        for entry in list(active):
            if entry[1] % LAG == 0:
                entry[2].pop(0)()
            entry[1] += 1
            if not entry[2]:
                active.remove(entry)
                ended.add(entry[0])
        if waiting:
            name = waiting.pop(0)
            steps = chunk_steps(*name)
            steps.pop(0)()
            active.append([name, 1, steps])

    def ticks(count):
        for _ in range(count):
            tick()

    def launch(b, m):
        grad_part(b, m)
        for c in range(chunks):
            pair_copy(b, m, c).start()
            waiting.append((b, m, c))

    def finish(b, *which):
        while any((b, m, c) not in ended for m in which for c in range(chunks)):
            tick()

    for name in ("k0", "w1", "w3"):
        loads[name].wait()
    round_weights(GATE)
    round_weights(UP)
    keys_part(0)
    loads["v0"].wait()
    scaled_part(0)
    loads["w2"].wait()
    round_weights(OUT)
    back_part(0)
    pl.semaphore_wait(barrier, head_count + 1 + jnp.where(depth > 0, 1, 0))
    launch(0, GATE)
    launch(0, UP)
    ticks(2)
    launch(0, OUT)
    for name in [name for name in loads if name[0] in "kvq" and name not in ("k0", "v0")]:
        loads[name].wait()
    for b in range(1, blocks):
        ticks(chunks)
        scaled_part(b)
        finish(b - 1, GATE, UP)
        keys_part(b)
        launch(b, OUT)
        finish(b - 1, OUT)
        ticks(1)
        back_part(b)
        launch(b, GATE)
        launch(b, UP)
        ticks(2)
        for i in range(tokens // tile):
            query_part(b - 1, i)
            tick()
        for part in out_parts(b - 1):
            part()
            tick()
    finish(blocks - 1, OUT, GATE)
    for i in range(tokens // tile):
        query_part(blocks - 1, i)
        tick()
    finish(blocks - 1, UP)
    for part in out_parts(blocks - 1):
        part()

    for b in range(blocks):
        for m in range(3):
            for c in range(chunks):
                pair_copy(b, m, c).wait_send()
                cross_copy(b, m, c).wait_send()
                mate_copy(b, m, c, core).wait_send()

                @pl.when(depth > 0)
                def _():
                    outward_copy(b, m, c).wait_send()

        for p in range(pieces):
            out_own(b, p).wait()
            for step in range(1, head_count):
                other = lax.rem(head + step, head_count)
                out_copy(b, other, p).wait_send()
                out_arrival(b, other, p).wait_recv()


def local(tok_count, head_count, queries, key_tokens, values, learn_rates, w_first, w_second, w_third):
    blocks, tokens, width = queries.shape
    inner = w_first.shape[1]
    half = inner // CORES
    chunks = next(n for n in (CHUNKS, 2, 1) if half % (n * 16) == 0)
    slab = tokens // head_count
    pieces = 2 if slab % 256 == 0 else 1
    firsts = [w[0] for w in (w_first, w_second, w_third)]
    bf16, f32 = jnp.bfloat16, jnp.float32
    dma = pltpu.SemaphoreType.DMA
    body = functools.partial(kernel, tok_count, head_count, chunks, pieces, inner)
    hbm = pl.BlockSpec(memory_space=pl.ANY)
    return pl.pallas_call(
        body,
        out_shape=jax.ShapeDtypeStruct((blocks, tokens // head_count, width * head_count), bf16),
        in_specs=[hbm, hbm, hbm, pl.BlockSpec(memory_space=pltpu.VMEM), hbm, hbm, hbm],
        out_specs=hbm,
        scratch_shapes=[
            pltpu.VMEM((blocks, tokens, width), bf16),
            pltpu.VMEM((blocks, tokens, width), bf16),
            pltpu.VMEM((blocks, tokens, width), bf16),
            pltpu.VMEM((3, inner, width), f32),
            pltpu.VMEM((blocks + 1, 3, inner, width), bf16),
            pltpu.VMEM((tokens, inner), f32),
            pltpu.VMEM((tokens, inner), f32),
            pltpu.VMEM((tokens, width), bf16),
            pltpu.VMEM((tokens, inner), bf16),
            pltpu.VMEM((tokens, inner), bf16),
            pltpu.VMEM((tokens, inner), bf16),
            pltpu.VMEM((blocks, 3, inner, width), bf16),
            pltpu.VMEM((blocks, 3, half, width), bf16),
            pltpu.VMEM((blocks, 3, half, width), bf16),
            pltpu.VMEM((blocks, 3, half, width), bf16),
            pltpu.VMEM((blocks, 3, half, width), bf16),
            pltpu.VMEM((3, half, width), f32),
            pltpu.VMEM((3, half, width), f32),
            pltpu.VMEM((blocks, tokens, width), bf16),
            dma((3 + 3 * blocks,)),
        ]
        + [dma((3 * blocks, chunks)) for _ in range(9)]
        + [dma((blocks * pieces, head_count)) for _ in range(2)],
        compiler_params=pltpu.CompilerParams(
            collective_id=0, has_side_effects=True, vmem_limit_bytes=56 * 1024 * 1024
        ),
    )(queries, key_tokens, values, learn_rates, *firsts)


def solution(mesh):
    placed = (
        P(None, ("grp", "tok"), "head"),
        P(None, ("grp", "tok"), "head"),
        P(None, ("grp", "tok"), "head"),
        P(None, "head", ("grp", "tok")),
        P("head", None, None),
        P("head", None, None),
        P("head", None, None),
    )
    return jax.shard_map(
        functools.partial(local, mesh.shape["tok"], mesh.shape["head"]),
        mesh=mesh,
        in_specs=placed,
        out_specs=P(None, ("grp", "tok", "head"), None),
        check_vma=False,
    )
```

time: 205 us -> 103 us (0.50)
  waiting for transfers between devices: 137 us -> 0 us
  Pallas kernels: 0 us -> 101 us
  matrix products: 27.1 us -> 0 us
  between operations: 13.4 us -> 0.01 us
  local copies, waits for them, and re-layouts: 14.2 us -> 2.46 us
  starting transfers between devices: 7.33 us -> 0 us
  other arithmetic: 5.36 us -> 0 us
    pallas_call x0 -> x1, Pallas kernels: none -> 101 us  [local(): pl.pallas_call(body, out_shape=jax.ShapeDtypeStruct((blocks, tokens // he...]
    unnamed x6 -> x0, waiting for transfers between devices: 75.5 us -> none
    all_gather x2 -> x0, waiting for transfers between devices: 53.1 us -> none  [local(): lax.all_gather(current.astype(jnp.bfloat16), 'tok', axis=0, tiled=True)]
    dot_general x16 -> x0, matrix products: 27.1 us -> none  [the longest x2 7.47 us: apply_weights(): lax.dot_general(hidden, second_b, CONTRACT_LAST, preferred_element_type=j...]
    all_to_all x2 -> x0, waiting for transfers between devices: 8.93 us -> none  [local(): lax.all_to_all(produced, 'head', split_axis=0, concat_axis=1, tiled=True)]
    unnamed x28 -> x1, local copies, waits for them, and re-layouts: 10.9 us -> 2.46 us
    all_to_all x2 -> x0, starting transfers between devices: 7.02 us -> none  [local(): lax.all_to_all(produced, 'head', split_axis=0, concat_axis=1, tiled=True)]
    convert_element_type x4 -> x0, other arithmetic: 2.58 us -> none  [the longest x2 1.78 us: local(): current.astype(jnp.bfloat16)]
  transfers between devices with their start and end apart: 6 -> 0, of which waited for: 5 -> 0; matrix products, arithmetic and copies ran while one was open for 7% -> 0% of each run, Pallas kernels for 0% -> 0%
where the time goes in v2:
time: 103 us
  Pallas kernels  101 us (98%)
  local copies, waits for them, and re-layouts  2.46 us (2%)
    pallas_call x1, Pallas kernels, local(): pl.pallas_call(body, out_shape=jax.ShapeDtypeStruct((blocks, tokens // he...  101 us
    unnamed x1, local copies, waits for them, and re-layouts  2.46 us

profile of v2, /device:TPU:0, one launch (start us, length us, event | category | flops | bytes accessed | tf_op | source)
XLA Modules:
  0.0 103.1 jit_solution(5929489172342960218)
XLA Ops:
  0.0 100.6 %shard_map.73 = bf16[2,256,1280]{2,1,0:T(8,128)(2,1)} custom-call(bf16[2,512,640]{2,1,0:T(8,128)(2,1)} %q_hbm.1, bf16[2,512,640]{2,1,0:T(8,128)(2,1)} %k_hbm.1, bf16[2,512,640]{2,1,0:T(8,128)(2,1)} %v_hbm.1, f32[2,1,512]{2,1,0:T(1,128)} %rates_ref.1, f32[640,640]{1,0:T(8,128)} %bitcast.3, f32[640,640]{1,0:T(8,128)} %bitcast.4, f32[640,640]{1,0:T(8,128)} %bitcast.5), custom_call_target="tpu_custom_call" | custom-call | tf_op jit(solution)/shard_map/pallas_call | solution.py:387
  100.6 2.5 %copy.9 = bf16[2,256,1280]{2,1,0:T(8,128)(2,1)} copy(bf16[2,256,1280]{2,1,0:T(8,128)(2,1)} %shard_map.73) | data formatting | bytes 2621440
